TPU v7x, 512 devices: a whole 4x4x16 slice. The times are simulated.
512 devices in a mesh: tm: 128 (over z, y, core), head: 4 (over x).
Axes of the slice: x: 4, y: 4, z: 16, core: 2. Of those that a mesh axis runs over, the one named last changes fastest.
Arguments:
- queries: bfloat16 [128, 384, 24, 128], P('tm', None, 'head'), may hold values from -40 to 40
- key_vectors: bfloat16 [128, 384, 24, 128], P('tm', None, 'head'), may hold values from -40 to 40
- value_vectors: bfloat16 [128, 384, 24, 128], P('tm', None, 'head'), may hold values from -6 to 6
- head_class: int32 [24], replicated, may hold values from 0 to 1, as said below
- frame_mask: int32 [4, 4], replicated, may hold values from 0 to 1, as said below
Outputs:
- attended: bfloat16 [128, 384, 24, 128], P('tm', None, 'head')
Inputs may be any that keep to these rules, and one draw needn't show every extreme that they name: `head_class`: head group g holds heads g * 6 to g * 6 + 5; each group holds 1 or 5 temporal heads, and groups 2k and 2k + 1 hold 6 temporal heads together. `frame_mask`: the diagonal is all ones.
All inputs are finite; a program needn't handle non-finite values.
Results may differ from a plain program's by a relative error of at most 0.0042.
Values may be sent and summed in bfloat16 or wider, within the bound.
A program may use at most 64 MiB of HBM per device.

v0:
```python
import jax
import jax.numpy as jnp
from jax import lax
from jax.sharding import PartitionSpec as P


def frame_attend(triple):
    query_block, key_block, value_block = triple
    score_scale = query_block.shape[-1] ** (-0.5)
    scores = (
        jnp.einsum("id,jd->ij", query_block, key_block, preferred_element_type=jnp.float32)
        * score_scale
    )
    peak = jnp.max(scores, axis=-1, keepdims=True)
    exponent = jnp.exp(scores - peak)
    totals = jnp.sum(exponent, axis=-1, keepdims=True)
    blended = jnp.dot(
        exponent.astype(jnp.bfloat16), value_block, preferred_element_type=jnp.float32
    )
    return (blended / totals).astype(jnp.bfloat16)


def run_spatial(triple):
    moved = tuple((jnp.moveaxis(a[0], 1, 0) for a in triple))
    blended = lax.map(frame_attend, moved)
    return jnp.moveaxis(blended, 0, 1)[None]


def run_temporal(triple, frame_mask):
    query_block = lax.all_to_all(triple[0], "tm", split_axis=1, concat_axis=0, tiled=True)
    key_block = lax.all_to_all(triple[1], "tm", split_axis=1, concat_axis=0, tiled=True)
    value_block = lax.all_to_all(triple[2], "tm", split_axis=1, concat_axis=0, tiled=True)
    score_scale = query_block.shape[-1] ** (-0.5)
    frame_total = query_block.shape[0]
    block_total = frame_mask.shape[0]
    frame_block = jnp.arange(frame_total, dtype=jnp.int32) // (frame_total // block_total)
    onehot = (frame_block[:, None] == jnp.arange(block_total, dtype=jnp.int32)[None, :]).astype(
        jnp.float32
    )
    allowed = jnp.dot(jnp.dot(onehot, frame_mask.astype(jnp.float32)), onehot.T) > 0.5
    scores = (
        jnp.einsum("fpmd,gpmd->pmfg", query_block, key_block, preferred_element_type=jnp.float32)
        * score_scale
    )
    scores = jnp.where(allowed, scores, jnp.float32(-1e30))
    peak = jnp.max(scores, axis=-1, keepdims=True)
    exponent = jnp.where(allowed, jnp.exp(scores - peak), jnp.float32(0.0))
    totals = jnp.sum(exponent, axis=-1)
    blended = jnp.einsum(
        "pmfg,gpmd->fpmd",
        exponent.astype(jnp.bfloat16),
        value_block,
        preferred_element_type=jnp.float32,
    )
    result = (blended / jnp.transpose(totals, (2, 0, 1))[..., None]).astype(jnp.bfloat16)
    return lax.all_to_all(result, "tm", split_axis=0, concat_axis=1, tiled=True)


def per_device(queries, key_vectors, value_vectors, head_class, frame_mask):
    group_heads = queries.shape[2]
    moved_heads = group_heads // 3
    half_heads = group_heads // 2
    least_count = half_heads - moved_heads
    most_count = half_heads + moved_heads
    head_group = lax.axis_index("head")
    local_class = lax.dynamic_slice_in_dim(head_class, head_group * group_heads, group_heads)
    sorted_heads = jnp.argsort(local_class, stable=True)
    head_rank = jnp.argsort(sorted_heads)
    temporal_count = jnp.sum(local_class)
    position = jnp.arange(group_heads, dtype=jnp.int32)
    spatial_in = tuple(
        (
            jnp.take(a, sorted_heads[:most_count], axis=2)
            for a in (queries, key_vectors, value_vectors)
        )
    )
    temporal_in = tuple(
        (
            jnp.take(a, sorted_heads[least_count:], axis=2)
            for a in (queries, key_vectors, value_vectors)
        )
    )
    spatial_out = run_spatial(spatial_in)
    temporal_out = run_temporal(temporal_in, frame_mask)
    result_pool = jnp.concatenate([spatial_out, temporal_out], axis=2)
    slot_index = jnp.where(
        position < group_heads - temporal_count, position, most_count + position - least_count
    )
    return jnp.take(result_pool, jnp.take(slot_index, head_rank), axis=2)


def solution(mesh):
    return jax.shard_map(
        per_device,
        mesh=mesh,
        in_specs=(
            P("tm", None, "head", None),
            P("tm", None, "head", None),
            P("tm", None, "head", None),
            P(),
            P(),
        ),
        out_specs=P("tm", None, "head", None),
        check_vma=False,
    )
```

profile of v0, /device:TPU:1, one launch (start us, length us, event | category | flops | bytes accessed | tf_op | source)
XLA Modules:
  0.0 223.3 jit_solution(13446374098697318869)
XLA Ops:
  1.4 1.0 sort.34
  2.5 1.8 gather_fusion.6
  5.5 1.0 bitcast_select_fusion.2
  6.5 1.2 copy.42
  7.8 20.7 %all-to-all-start.2 = ((bf16[1,384,5,128]{3,2,0,1:T(8,128)(2,1)}), bf16[1,384,5,128]{3,2,0,1:T(8,128)(2,1)S(1)}, u32[]{:S(2)}, u32[]{:S(2)}) async-start(bf16[1,384,5,128]{3,2,0,1:T(8,128)(2,1)} %copy.42), calls=%async_computation.2 | async-start | bytes 1572864 | tf_op jit(solution)/shard_map/all_to_all | solution.py:31
  28.5 1.3 copy.40
  29.7 40.1 %all-to-all-done.2 = bf16[1,384,5,128]{3,2,0,1:T(8,128)(2,1)S(1)} async-done(((bf16[1,384,5,128]{3,2,0,1:T(8,128)(2,1)}), bf16[1,384,5,128]{3,2,0,1:T(8,128)(2,1)S(1)}, u32[]{:S(2)}, u32[]{:S(2)}) %all-to-all-start.2) | async-done | bytes 491552 | tf_op jit(solution)/shard_map/all_to_all | solution.py:31
  69.9 9.9 %all-to-all-start.1 = ((bf16[1,384,5,128]{3,2,0,1:T(8,128)(2,1)}), bf16[1,384,5,128]{3,2,0,1:T(8,128)(2,1)}, u32[]{:S(2)}, u32[]{:S(2)}) async-start(bf16[1,384,5,128]{3,2,0,1:T(8,128)(2,1)} %copy.40), calls=%async_computation.1 | async-start | bytes 1572864 | tf_op jit(solution)/shard_map/all_to_all | solution.py:30
  79.8 1.3 copy.37
  81.1 39.8 %all-to-all-done.1 = bf16[1,384,5,128]{3,2,0,1:T(8,128)(2,1)} async-done(((bf16[1,384,5,128]{3,2,0,1:T(8,128)(2,1)}), bf16[1,384,5,128]{3,2,0,1:T(8,128)(2,1)}, u32[]{:S(2)}, u32[]{:S(2)}) %all-to-all-start.1) | async-done | bytes 491552 | tf_op jit(solution)/shard_map/all_to_all | solution.py:30
  120.9 9.9 %all-to-all-start = ((bf16[1,384,5,128]{3,2,0,1:T(8,128)(2,1)}), bf16[1,384,5,128]{3,2,0,1:T(8,128)(2,1)}, u32[]{:S(2)}, u32[]{:S(2)}) async-start(bf16[1,384,5,128]{3,2,0,1:T(8,128)(2,1)} %copy.37), calls=%async_computation | async-start | bytes 1572864 | tf_op jit(solution)/shard_map/all_to_all | solution.py:32
  136.0 1.0 fusion.24
  137.1 1.6 fusion.20
  139.0 33.0 %all-to-all-done = bf16[1,384,5,128]{3,2,0,1:T(8,128)(2,1)} async-done(((bf16[1,384,5,128]{3,2,0,1:T(8,128)(2,1)}), bf16[1,384,5,128]{3,2,0,1:T(8,128)(2,1)}, u32[]{:S(2)}, u32[]{:S(2)}) %all-to-all-start) | async-done | bytes 491552 | tf_op jit(solution)/shard_map/all_to_all | solution.py:32
  171.9 1.6 fusion.21
  173.5 1.4 copy.48
  174.9 9.6 %all-to-all-start.3 = ((bf16[128,3,5,128]{3,1,2,0:T(4,128)(2,1)}), bf16[128,3,5,128]{3,1,2,0:T(4,128)(2,1)S(1)}, u32[]{:S(2)}, u32[]{:S(2)}) async-start(bf16[128,3,5,128]{3,1,2,0:T(4,128)(2,1)} %copy.48), calls=%async_computation.3 | async-start | bytes 1310720 | tf_op jit(solution)/shard_map/all_to_all | solution.py:56
  184.5 8.1 %while.10 = (s32[]{:T(128)}, bf16[5,384,128]{2,1,0:T(8,128)(2,1)S(1)}, bf16[5,384,128]{2,1,0:T(8,128)(2,1)S(1)}, bf16[5,384,128]{2,1,0:T(8,128)(2,1)S(1)}, bf16[5,384,128]{2,1,0:T(8,128)(2,1)}, /*index=5*/s32[]{:T(128)}) while((s32[]{:T(128)}, bf16[5,384,128]{2,1,0:T(8,128)(2,1)S(1)}, bf16[5,384,128]{2,1,0:T(8,128)(2,1)S(1)}, ...), condition=%wide.region_6.8_spmd, body=%wide.region_3.0_spmd.sunk | while | flops 76479744 | bytes 2173517 | solution.py:25
  184.9 1.2 fusion.51
  186.6 1.2 fusion.51
  188.2 1.2 fusion.51
  189.8 1.2 fusion.51
  191.5 1.2 fusion.51
  192.7 28.3 %all-to-all-done.3 = bf16[128,3,5,128]{3,1,2,0:T(4,128)(2,1)S(1)} async-done(((bf16[128,3,5,128]{3,1,2,0:T(4,128)(2,1)}), bf16[128,3,5,128]{3,1,2,0:T(4,128)(2,1)S(1)}, u32[]{:S(2)}, u32[]{:S(2)}) %all-to-all-start.3) | async-done | bytes 491552 | tf_op jit(solution)/shard_map/all_to_all | solution.py:56
  (55 shorter events, 12.0 us)
Async XLA Ops:
  0.0 4.9 %copy-start = (bf16[1,384,6,128]{3,1,2,0:T(8,128)(2,1)S(1)}, bf16[1,384,6,128]{3,1,2,0:T(8,128)(2,1)}, u32[]{:S(2)}) copy-start(bf16[1,384,6,128]{3,1,2,0:T(8,128)(2,1)} %param.11) | copy-start | bytes 1769476
  0.0 0.7 copy-start.7
  2.4 1.8 copy-start.1
  7.8 20.7 %copy-start.3 = (bf16[1,384,5,128]{3,1,2,0:T(8,128)(2,1)S(1)}, bf16[1,384,5,128]{3,1,2,0:T(8,128)(2,1)}, u32[]{:S(2)}) copy-start(bf16[1,384,5,128]{3,1,2,0:T(8,128)(2,1)} %get-tuple-element.63) | copy-start | bytes 1474564
  7.8 62.1 %all-to-all-start.2 = ((bf16[1,384,5,128]{3,2,0,1:T(8,128)(2,1)}), bf16[1,384,5,128]{3,2,0,1:T(8,128)(2,1)S(1)}, u32[]{:S(2)}, u32[]{:S(2)}) async-start(bf16[1,384,5,128]{3,2,0,1:T(8,128)(2,1)} %copy.42), calls=%async_computation.2 | async-start | bytes 1572864 | tf_op jit(solution)/shard_map/all_to_all | solution.py:31
  69.9 9.9 %copy-start.4 = (bf16[1,384,5,128]{3,2,0,1:T(8,128)(2,1)}, bf16[1,384,5,128]{3,2,0,1:T(8,128)(2,1)S(1)}, u32[]{:S(2)}) copy-start(bf16[1,384,5,128]{3,2,0,1:T(8,128)(2,1)S(1)} %all-to-all-done.2) | copy-start | bytes 1474564
  69.9 51.0 %all-to-all-start.1 = ((bf16[1,384,5,128]{3,2,0,1:T(8,128)(2,1)}), bf16[1,384,5,128]{3,2,0,1:T(8,128)(2,1)}, u32[]{:S(2)}, u32[]{:S(2)}) async-start(bf16[1,384,5,128]{3,2,0,1:T(8,128)(2,1)} %copy.40), calls=%async_computation.1 | async-start | bytes 1572864 | tf_op jit(solution)/shard_map/all_to_all | solution.py:30
  120.9 51.0 %all-to-all-start = ((bf16[1,384,5,128]{3,2,0,1:T(8,128)(2,1)}), bf16[1,384,5,128]{3,2,0,1:T(8,128)(2,1)}, u32[]{:S(2)}, u32[]{:S(2)}) async-start(bf16[1,384,5,128]{3,2,0,1:T(8,128)(2,1)} %copy.37), calls=%async_computation | async-start | bytes 1572864 | tf_op jit(solution)/shard_map/all_to_all | solution.py:32
  131.5 1.1 copy-start.2
  132.5 0.7 copy-start.8
  136.0 1.1 copy-start.5
  174.9 9.6 %copy-start.6 = (bf16[5,384,128]{2,1,0:T(8,128)(2,1)S(1)}, bf16[5,384,128]{2,1,0:T(8,128)(2,1)}, u32[]{:S(2)}) copy-start(bf16[5,384,128]{2,1,0:T(8,128)(2,1)} %custom-call.16) | copy-start | bytes 1474564
  174.9 46.1 %all-to-all-start.3 = ((bf16[128,3,5,128]{3,1,2,0:T(4,128)(2,1)}), bf16[128,3,5,128]{3,1,2,0:T(4,128)(2,1)S(1)}, u32[]{:S(2)}, u32[]{:S(2)}) async-start(bf16[128,3,5,128]{3,1,2,0:T(4,128)(2,1)} %copy.48), calls=%async_computation.3 | async-start | bytes 1310720 | tf_op jit(solution)/shard_map/all_to_all | solution.py:56
where the time goes:
time: 226 us; the launch traced here: 223 us
  waiting for transfers between devices  141 us (62%)
  starting transfers between devices  50.1 us (22%)
  local copies, waits for them, and re-layouts  13.4 us (6%)
  matrix products  11 us (5%)
  other arithmetic  6.56 us (3%)
    all_to_all x1, waiting for transfers between devices, run_temporal(): lax.all_to_all(triple[1], 'tm', split_axis=1, concat_axis=0, tiled=True)  40.1 us
    all_to_all x1, waiting for transfers between devices, run_temporal(): lax.all_to_all(triple[0], 'tm', split_axis=1, concat_axis=0, tiled=True)  39.8 us
    all_to_all x1, waiting for transfers between devices, run_temporal(): lax.all_to_all(triple[2], 'tm', split_axis=1, concat_axis=0, tiled=True)  33 us
    all_to_all x1, waiting for transfers between devices, run_temporal(): return lax.all_to_all(result, 'tm', split_axis=0, concat_axis=1, tiled=True)  28.3 us
    all_to_all x1, starting transfers between devices, run_temporal(): lax.all_to_all(triple[1], 'tm', split_axis=1, concat_axis=0, tiled=True)  20.7 us
    all_to_all x1, starting transfers between devices, run_temporal(): lax.all_to_all(triple[0], 'tm', split_axis=1, concat_axis=0, tiled=True)  9.9 us
    all_to_all x1, starting transfers between devices, run_temporal(): lax.all_to_all(triple[2], 'tm', split_axis=1, concat_axis=0, tiled=True)  9.89 us
    all_to_all x1, starting transfers between devices, run_temporal(): return lax.all_to_all(result, 'tm', split_axis=0, concat_axis=1, tiled=True)  9.62 us
  transfers between devices with their start and end apart: 4, of which 4 were waited for; matrix products, arithmetic and copies ran while one was open for 8% of the time, Pallas kernels for 0%

commit v1 on v0

v1 whole, which is shorter than its diff:
```python
import functools

import jax
import jax.numpy as jnp
from jax import lax
from jax.experimental import pallas as pl
from jax.experimental.pallas import tpu as pltpu
from jax.sharding import PartitionSpec as P

MESH = pl.DeviceIdType.MESH
ROWS = 8
SLOTS = 3
SIDE = 8


def attend(query, key, value, scale, allowed=None):
    scores = (
        lax.dot_general(query, key, (((1,), (1,)), ((), ())), preferred_element_type=jnp.float32)
        * scale
    )
    if allowed is not None:
        scores = jnp.where(allowed, scores, jnp.float32(-1e30))
    peak = jnp.max(scores, axis=-1, keepdims=True)
    exponent = jnp.exp(scores - peak)
    if allowed is not None:
        exponent = jnp.where(allowed, exponent, jnp.float32(0.0))
    totals = jnp.sum(exponent, axis=-1, keepdims=True)
    blended = jnp.dot(exponent.astype(jnp.bfloat16), value, preferred_element_type=jnp.float32)
    return blended / totals


def worker_core(slot, y_rel):
    return jnp.where(
        slot == 0, 0, jnp.where(slot == 1, (y_rel != 0).astype(jnp.int32), (y_rel != 3).astype(jnp.int32))
    )


def z_step(count, n):
    half = (n + 1) // 2
    return jnp.where(lax.rem(n, 2) == 1, count // 2 - half, lax.rem(count // 2 + half, count))


def kernel(
    class_ref, mask_ref, q_hbm, k_hbm, v_hbm, out_ref,
    own, tsend, wsend, wrecv, rx, wide, blend, rsend, res, bsend,
    load_sem, wsend_sem, wrecv_sem, tsend_sem, trecv_sem, rsend_sem, rrecv_sem, bsend_sem, brecv_sem,
):
    me = lax.axis_index("tm")
    group = lax.axis_index("head")
    frames = rx.shape[1]
    heads = own.shape[1]
    tiles = own.shape[2]
    patches = tiles * ROWS
    depth = own.shape[-1]
    z_count = frames // SIDE
    per_z = tiles // z_count
    scale = depth ** (-0.5)
    z, y, core = me // SIDE, lax.rem(me // 2, 4), lax.rem(me, 2)
    partner = {"head": group + 1 - 2 * lax.rem(group, 2)}

    loads = [
        pltpu.make_async_copy(src, own.at[a], load_sem.at[a])
        for a, src in enumerate((q_hbm, k_hbm, v_hbm))
    ]
    for load in loads:
        load.start()

    barrier = pltpu.get_barrier_semaphore()
    pl.semaphore_signal(barrier, inc=1, device_id=partner, device_id_type=MESH)

    def greet(k, carry):
        pl.semaphore_signal(
            barrier, inc=1, device_id={"tm": lax.rem(me + k, frames)}, device_id_type=MESH
        )
        return carry

    lax.fori_loop(1, frames, greet, 0)

    classes = [class_ref[group * heads + h] for h in range(heads)]
    count = functools.reduce(lambda a, b: a + b, classes)
    heavy = count > heads // 2
    odd = jnp.int32(0)
    for h in range(heads):
        odd = odd + jnp.where(heavy, 1 - classes[h], classes[h]) * h

    def major(k):
        return k + (odd <= k).astype(jnp.int32)

    for load in loads:
        load.wait()

    first_t = jnp.where(heavy, major(0), odd)
    for a in range(3):
        tsend[0, :, a] = own[a, first_t]
    for s in range(SLOTS - 1):
        for a in range(3):
            wsend[s, a] = own[a, major(3 + s)]

    pl.semaphore_wait(barrier, frames)

    swaps = [
        pltpu.make_async_remote_copy(
            wsend.at[s], wrecv.at[s], wsend_sem.at[s], wrecv_sem.at[s],
            device_id=partner, device_id_type=MESH,
        )
        for s in range(SLOTS - 1)
    ]
    for swap in swaps:
        swap.start()

    def spread(slot):
        def body(n, carry):
            zz = lax.rem(z + z_step(z_count, n // per_z), z_count)
            i = lax.rem(n, per_z)
            y_rel = lax.rem(slot + 1 + i, 4)
            yy = lax.rem(zz + y_rel, 4)
            to = zz * SIDE + yy * 2 + worker_core(slot, y_rel)
            tile = zz * per_z + i
            src, dst = tsend.at[slot, tile], rx.at[slot // 2, me]

            @pl.when(to != me)
            def _():
                pltpu.make_async_remote_copy(
                    src, dst, tsend_sem.at[slot], trecv_sem.at[slot],
                    device_id={"tm": to}, device_id_type=MESH,
                ).start()

            @pl.when(to == me)
            def _():
                pltpu.make_async_copy(src, dst, trecv_sem.at[slot]).start()

            return carry

        lax.fori_loop(0, tiles, body, 0)

    def spatial(slot, triple):
        query, key, value = (x.reshape(patches, depth) for x in triple)
        step = 128
        for r in range(0, patches, step):
            part = attend(query[r : r + step], key, value, scale)
            res[SLOTS + slot, r // ROWS : (r + step) // ROWS] = part.reshape(
                step // ROWS, ROWS, depth
            ).astype(jnp.bfloat16)

    spread(0)
    for s in range(1, SLOTS):
        swaps[s - 1].wait_recv()
        for a in range(3):
            tsend[s, :, a] = jnp.where(heavy, own[a, major(s)], wrecv[s - 1, a])
        spread(s)

    first_s = jnp.where(heavy, odd, major(0))
    spatial(0, [own[a, first_s] for a in range(3)])
    for s in range(1, SLOTS):
        spatial(s, [jnp.where(heavy, wrecv[s - 1, a], own[a, major(s)]) for a in range(3)])

    block_total = mask_ref.shape[0]
    row_block = lax.broadcasted_iota(jnp.int32, (frames, frames), 0) // (frames // block_total)
    col_block = lax.broadcasted_iota(jnp.int32, (frames, frames), 1) // (frames // block_total)
    kept = jnp.zeros((frames, frames), jnp.int32)
    for r in range(block_total):
        for c in range(block_total):
            kept = jnp.where((row_block == r) & (col_block == c), mask_ref[r, c], kept)
    allowed = kept == 1

    y_mine = lax.rem(y - lax.rem(z, 4) + 4, 4)

    def role(slot):
        i = lax.rem(y_mine - slot + 3, 4)
        return i, (i < per_z) & (core == worker_core(slot, y_mine))

    def temporal(slot, carry):
        i, mine = role(slot)

        @pl.when(mine)
        def _():
            half = slot // 2
            pltpu.make_async_copy(rx.at[half], rx.at[half], trecv_sem.at[slot]).wait()
            for a in range(3):
                wide[a] = rx[half, :, a].astype(jnp.float32).reshape(frames * ROWS, depth)
            for p in range(ROWS):
                rows = pl.ds(p, frames, stride=ROWS)
                query, key, value = (wide[a, rows, :].astype(jnp.bfloat16) for a in range(3))
                blend[rows, :] = attend(query, key, value, scale, allowed)
            rsend[half] = blend[...].reshape(frames, ROWS, depth).astype(jnp.bfloat16)
            tile = z * per_z + i

            def body(n, c):
                to = lax.rem(z + z_step(z_count, n // SIDE), z_count) * SIDE + lax.rem(me + n, SIDE)
                src, dst = rsend.at[half, to], res.at[slot, tile]

                @pl.when(to != me)
                def _():
                    pltpu.make_async_remote_copy(
                        src, dst, rsend_sem.at[slot], rrecv_sem.at[slot],
                        device_id={"tm": to}, device_id_type=MESH,
                    ).start()

                @pl.when(to == me)
                def _():
                    pltpu.make_async_copy(src, dst, rrecv_sem.at[slot]).start()

                return c

            lax.fori_loop(0, frames, body, 0)

        return carry

    lax.fori_loop(0, SLOTS, temporal, 0)

    backs = []
    for s in range(1, SLOTS):
        pltpu.make_async_copy(res.at[s], res.at[s], rrecv_sem.at[s]).wait()
        bsend[s - 1] = jnp.where(heavy, res[SLOTS + s], res[s])
        back = pltpu.make_async_remote_copy(
            bsend.at[s - 1], res.at[2 * SLOTS - 1 + s], bsend_sem.at[s - 1], brecv_sem.at[s - 1],
            device_id=partner, device_id_type=MESH,
        )
        back.start()
        backs.append(back)

    pltpu.make_async_copy(res.at[0], res.at[0], rrecv_sem.at[0]).wait()

    for swap in swaps:
        swap.wait_send()
    for s in range(SLOTS):
        _, mine = role(s)

        @pl.when(mine)
        def _():
            most = tsend.at[s, pl.ds(0, tiles - 1)]
            pltpu.make_async_copy(most, most, tsend_sem.at[s]).wait()
            rest = rsend.at[s // 2, pl.ds(0, frames - 1)]
            pltpu.make_async_copy(rest, rest, rsend_sem.at[s]).wait()

        @pl.when(jnp.logical_not(mine))
        def _():
            pltpu.make_async_copy(tsend.at[s], tsend.at[s], tsend_sem.at[s]).wait()

    for back in backs:
        back.wait()

    for h in range(heads):
        k = h - (odd < h).astype(jnp.int32)
        from_major = jnp.where(k < SLOTS, jnp.where(heavy, k, SLOTS + k), SLOTS + k)
        from_odd = jnp.where(heavy, SLOTS, 0)
        out_ref[h] = res[jnp.where(odd == h, from_odd, from_major)]


def per_device(queries, key_vectors, value_vectors, head_class, frame_mask):
    _, patches, heads, depth = queries.shape
    frames = lax.axis_size("tm")
    tiles = patches // ROWS
    by_head = [
        jnp.transpose(a[0], (1, 0, 2)).reshape(heads, tiles, ROWS, depth)
        for a in (queries, key_vectors, value_vectors)
    ]
    bf16, f32 = jnp.bfloat16, jnp.float32
    tile = (ROWS, depth)
    dma = pltpu.SemaphoreType.DMA
    out = pl.pallas_call(
        kernel,
        out_shape=jax.ShapeDtypeStruct((heads, tiles, ROWS, depth), bf16),
        in_specs=[pl.BlockSpec(memory_space=pltpu.SMEM)] * 2 + [pl.BlockSpec(memory_space=pl.ANY)] * 3,
        out_specs=pl.BlockSpec(memory_space=pltpu.VMEM),
        scratch_shapes=[
            pltpu.VMEM((3, heads, tiles) + tile, bf16),
            pltpu.VMEM((SLOTS, tiles, 3) + tile, bf16),
            pltpu.VMEM((SLOTS - 1, 3, tiles) + tile, bf16),
            pltpu.VMEM((SLOTS - 1, 3, tiles) + tile, bf16),
            pltpu.VMEM((2, frames, 3) + tile, bf16),
            pltpu.VMEM((3, frames * ROWS, depth), f32),
            pltpu.VMEM((frames * ROWS, depth), f32),
            pltpu.VMEM((2, frames) + tile, bf16),
            pltpu.VMEM((3 * SLOTS - 1, tiles) + tile, bf16),
            pltpu.VMEM((SLOTS - 1, tiles) + tile, bf16),
            dma((3,)),
            dma((SLOTS - 1,)),
            dma((SLOTS - 1,)),
            dma((SLOTS,)),
            dma((SLOTS,)),
            dma((SLOTS,)),
            dma((SLOTS,)),
            dma((SLOTS - 1,)),
            dma((SLOTS - 1,)),
        ],
        compiler_params=pltpu.CompilerParams(
            collective_id=0, has_side_effects=True, vmem_limit_bytes=40 * 2**20
        ),
        name="split_heads_attention",
    )(head_class, frame_mask, *by_head)
    return jnp.transpose(out.reshape(heads, patches, depth), (1, 0, 2))[None]


def solution(mesh):
    spec = P("tm", None, "head", None)
    return jax.shard_map(
        per_device,
        mesh=mesh,
        in_specs=(spec, spec, spec, P(), P()),
        out_specs=spec,
        check_vma=False,
    )
```

time: 226 us -> 84.7 us (0.37); the launches traced: 223 us -> 84.4 us
  waiting for transfers between devices: 141 us -> 0 us
  Pallas kernels: 0 us -> 79.7 us
  starting transfers between devices: 50.1 us -> 0 us
  matrix products: 11 us -> 0 us
  local copies, waits for them, and re-layouts: 13.4 us -> 4.69 us
  other arithmetic: 6.56 us -> 0 us
    all_to_all x4 -> x0, waiting for transfers between devices: 141 us -> none  [the longest x1 40.1 us: run_temporal(): lax.all_to_all(triple[1], 'tm', split_axis=1, concat_axis=0, tiled=True)]
    pallas_call x0 -> x1, Pallas kernels: none -> 79.7 us  [per_device(): pl.pallas_call(kernel, out_shape=jax.ShapeDtypeStruct((heads, tiles, ROWS...]
    all_to_all x4 -> x0, starting transfers between devices: 50.1 us -> none  [the longest x1 20.7 us: run_temporal(): lax.all_to_all(triple[1], 'tm', split_axis=1, concat_axis=0, tiled=True)]
    dot_general x13 -> x0, matrix products: 11 us -> none  [the longest x5 5.99 us: frame_attend(): jnp.dot(exponent.astype(jnp.bfloat16), value_block, preferred_element_typ...]
    gather x8 -> x0, local copies, waits for them, and re-layouts: 6.28 us -> none  [the longest x3 3.05 us: per_device(): jnp.take(a, sorted_heads[least_count:], axis=2)]
    select_n x3 -> x0, local copies, waits for them, and re-layouts: 3.75 us -> none  [per_device(): jnp.take(a, sorted_heads[least_count:], axis=2)]
    unnamed x18 -> x11, local copies, waits for them, and re-layouts: 1.28 us -> 4.69 us
  transfers between devices with their start and end apart: 4 -> 0, of which waited for: 4 -> 0; matrix products, arithmetic and copies ran while one was open for 8% -> 0% of each run, Pallas kernels for 0% -> 0%
where the time goes in v1:
time: 84.7 us; the launch traced here: 84.4 us
  Pallas kernels  79.7 us (94%)
  local copies, waits for them, and re-layouts  4.69 us (6%)
    pallas_call x1, Pallas kernels, per_device(): pl.pallas_call(kernel, out_shape=jax.ShapeDtypeStruct((heads, tiles, ROWS...  79.7 us
    unnamed x11, local copies, waits for them, and re-layouts  4.69 us

profile of v1, /device:TPU:1, one launch (start us, length us, event | category | flops | bytes accessed | tf_op | source)
XLA Modules:
  0.0 84.4 jit_solution(18233840225852179327)
XLA Ops:
  0.0 0.0 copy-start.3
  0.0 0.0 copy-start.4
  0.0 0.7 copy-done.3
  0.7 0.0 copy-done.4
  0.7 0.0 copy-start
  0.7 1.1 %copy-done = bf16[1,384,6,128]{3,1,2,0:T(8,128)(2,1)S(1)} copy-done((bf16[1,384,6,128]{3,1,2,0:T(8,128)(2,1)S(1)}, bf16[1,384,6,128]{3,1,2,0:T(8,128)(2,1)}, u32[]{:S(2)}) %copy-start) | copy-done | bytes 589848
  1.8 0.0 copy-start.1
  1.8 1.1 %copy-done.1 = bf16[1,384,6,128]{3,1,2,0:T(8,128)(2,1)S(1)} copy-done((bf16[1,384,6,128]{3,1,2,0:T(8,128)(2,1)S(1)}, bf16[1,384,6,128]{3,1,2,0:T(8,128)(2,1)}, u32[]{:S(2)}) %copy-start.1) | copy-done | bytes 589848
  2.8 0.0 copy-start.2
  2.8 1.1 %copy-done.2 = bf16[1,384,6,128]{3,1,2,0:T(8,128)(2,1)S(1)} copy-done((bf16[1,384,6,128]{3,1,2,0:T(8,128)(2,1)S(1)}, bf16[1,384,6,128]{3,1,2,0:T(8,128)(2,1)}, u32[]{:S(2)}) %copy-start.2) | copy-done | bytes 589848
  3.9 79.7 %split_heads_attention.1 = bf16[6,48,8,128]{3,2,1,0:T(8,128)(2,1)S(1)} custom-call(s32[24]{0:T(128)S(1)} %copy-done.4, s32[4,4]{1,0:T(4,128)S(1)} %copy-done.3, bf16[6,48,8,128]{3,2,1,0:T(8,128)(2,1)S(1)} %bitcast.21, bf16[6,48,8,128]{3,2,1,0:T(8,128)(2,1)S(1)} %bitcast.22, bf16[6,48,8,128]{3,2,1,0:T(8,128)(2,1)S(1)} %bitcast.23), custom_call_target="tpu_custom_call" | custom-call | tf_op jit(solution)/shard_map/split_heads_attention/pallas_call | solution.py:261
  83.6 0.8 copy.7
Async XLA Ops:
  0.0 0.7 copy-start.3
  0.0 0.7 copy-start.4
  0.7 1.1 %copy-start = (bf16[1,384,6,128]{3,1,2,0:T(8,128)(2,1)S(1)}, bf16[1,384,6,128]{3,1,2,0:T(8,128)(2,1)}, u32[]{:S(2)}) copy-start(bf16[1,384,6,128]{3,1,2,0:T(8,128)(2,1)} %param.5) | copy-start | bytes 1769476
  1.8 1.1 %copy-start.1 = (bf16[1,384,6,128]{3,1,2,0:T(8,128)(2,1)S(1)}, bf16[1,384,6,128]{3,1,2,0:T(8,128)(2,1)}, u32[]{:S(2)}) copy-start(bf16[1,384,6,128]{3,1,2,0:T(8,128)(2,1)} %param.6) | copy-start | bytes 1769476
  2.8 1.1 %copy-start.2 = (bf16[1,384,6,128]{3,1,2,0:T(8,128)(2,1)S(1)}, bf16[1,384,6,128]{3,1,2,0:T(8,128)(2,1)}, u32[]{:S(2)}) copy-start(bf16[1,384,6,128]{3,1,2,0:T(8,128)(2,1)} %param.7) | copy-start | bytes 1769476

commit v2 on v1

v2 whole, which is shorter than its diff:
```python
import functools

import jax
import jax.numpy as jnp
from jax import lax
from jax.experimental import pallas as pl
from jax.experimental.pallas import tpu as pltpu
from jax.sharding import PartitionSpec as P

MESH = pl.DeviceIdType.MESH
ROWS = 8
SLOTS = 3
SIDE = 8


def attend(query, key, value, scale, allowed=None):
    scores = (
        lax.dot_general(query, key, (((1,), (1,)), ((), ())), preferred_element_type=jnp.float32)
        * scale
    )
    if allowed is not None:
        scores = jnp.where(allowed, scores, jnp.float32(-1e30))
    peak = jnp.max(scores, axis=-1, keepdims=True)
    exponent = jnp.exp(scores - peak)
    if allowed is not None:
        exponent = jnp.where(allowed, exponent, jnp.float32(0.0))
    totals = jnp.sum(exponent, axis=-1, keepdims=True)
    blended = jnp.dot(exponent.astype(jnp.bfloat16), value, preferred_element_type=jnp.float32)
    return blended / totals


UNITS = ((0, 0), (0, 1), (1, 0), (1, 1), (1, 2), (2, 0), (2, 1), (2, 2), (0, 2))


def kernel(
    class_hbm, mask_hbm, q_hbm, k_hbm, v_hbm, out_ref,
    class_ref, mask_ref, own, tsend, wsend, wrecv, rx, wide, blend, rsend, res, bsend,
    load_sem, wsend_sem, wrecv_sem, tsend_sem, trecv_sem, rsend_sem, rrecv_sem, bsend_sem, brecv_sem,
):
    me = lax.axis_index("tm")
    group = lax.axis_index("head")
    frames = rx.shape[1]
    heads = own.shape[1]
    tiles = own.shape[2]
    patches = tiles * ROWS
    depth = own.shape[-1]
    z_count = frames // SIDE
    scale = depth ** (-0.5)
    z, y, core = me >> 3, (me >> 1) & 3, me & 1
    partner = {"head": group ^ 1}

    loads = [
        pltpu.make_async_copy(src, dst, load_sem.at[n])
        for n, (src, dst) in enumerate(
            (
                (class_hbm, class_ref),
                (q_hbm, own.at[0]),
                (k_hbm, own.at[1]),
                (v_hbm, own.at[2]),
                (mask_hbm, mask_ref),
            )
        )
    ]
    for load in loads:
        load.start()

    barrier = pltpu.get_barrier_semaphore()
    pl.semaphore_signal(barrier, inc=1, device_id=partner, device_id_type=MESH)

    def greet(n, carry):
        pl.semaphore_signal(
            barrier, inc=1, device_id={"tm": me ^ (frames - n)}, device_id_type=MESH
        )
        return carry

    lax.fori_loop(1, frames, greet, 0)

    for load in loads:
        load.wait()

    classes = [class_ref[group * heads + h] for h in range(heads)]
    count = functools.reduce(lambda a, b: a + b, classes)
    heavy = count > heads // 2
    odd = jnp.int32(0)
    for h in range(heads):
        odd = odd + jnp.where(heavy, 1 - classes[h], classes[h]) * h

    def major(k):
        return k + (odd <= k).astype(jnp.int32)

    def unit_rows(i):
        return pl.ds(i * z_count, z_count)

    def stage(unit):
        slot, i = UNITS[unit]
        for a in range(3):
            if slot == 0:
                block = own[a, jnp.where(heavy, major(0), odd), unit_rows(i)]
            else:
                block = jnp.where(heavy, own[a, major(slot), unit_rows(i)], wrecv[slot - 1, i, a])
            tsend[unit_rows(unit), a] = block

    def spatial(slot, triple):
        query, key, value = (x.reshape(patches, depth) for x in triple)
        step = 128
        for r in range(0, patches, step):
            part = attend(query[r : r + step], key, value, scale)
            res[SLOTS + slot, r // ROWS : (r + step) // ROWS] = part.reshape(
                step // ROWS, ROWS, depth
            ).astype(jnp.bfloat16)

    stage(0)
    for s in range(SLOTS - 1):
        for i in range(SLOTS):
            for a in range(3):
                wsend[s, i, a] = own[a, major(3 + s), unit_rows(i)]
    first_s = jnp.where(heavy, odd, major(0))
    spatial(0, [own[a, first_s] for a in range(3)])

    pl.semaphore_wait(barrier, frames)

    swaps = {
        (s, i): pltpu.make_async_remote_copy(
            wsend.at[s - 1, i], wrecv.at[s - 1, i], wsend_sem.at[s - 1, i], wrecv_sem.at[s - 1, i],
            device_id=partner, device_id_type=MESH,
        )
        for s in range(1, SLOTS)
        for i in range(SLOTS)
    }

    def spread(unit):
        half = 1 if unit == 1 else 0
        rank = max(unit - 1, 0)
        land, sem = rx.at[half, me], trecv_sem.at[half]
        first = unit * z_count

        def worker(zz):
            return zz * SIDE + ((zz + rank) & 3) * 2 + ((rank // 4 + (zz >> 2)) & 1)

        def send(zz):
            pltpu.make_async_remote_copy(
                tsend.at[first + zz], land, tsend_sem, sem,
                device_id={"tm": worker(zz)}, device_id_type=MESH,
            ).start()

        def body(n, carry):
            send(z ^ (z_count - n))
            return carry

        lax.fori_loop(1, z_count, body, 0)
        here = worker(z) == me

        @pl.when(here)
        def _():
            pltpu.make_async_copy(tsend.at[first + z], land, sem).start()

        @pl.when(jnp.logical_not(here))
        def _():
            send(z)

    block_total = mask_ref.shape[0]

    def temporal(unit, half):
        slot = jnp.where((unit < 2) | (unit == 8), 0, (unit + 1) // 3)
        i = jnp.where(unit < 2, unit, jnp.where(unit == 8, 2, lax.rem(unit + 1, 3)))
        row_block = lax.broadcasted_iota(jnp.int32, (frames, frames), 0) // (frames // block_total)
        col_block = lax.broadcasted_iota(jnp.int32, (frames, frames), 1) // (frames // block_total)
        kept = jnp.zeros((frames, frames), jnp.int32)
        for r in range(block_total):
            for c in range(block_total):
                kept = jnp.where((row_block == r) & (col_block == c), mask_ref[r, c], kept)
        allowed = kept == 1
        pltpu.make_async_copy(rx.at[half], rx.at[half], trecv_sem.at[half]).wait()
        for a in range(3):
            wide[a] = rx[half, :, a].astype(jnp.float32).reshape(frames * ROWS, depth)
        for p in range(ROWS):
            rows = pl.ds(p, frames, stride=ROWS)
            query, key, value = (wide[a, rows, :].astype(jnp.bfloat16) for a in range(3))
            blend[rows, :] = attend(query, key, value, scale, allowed)
        rsend[half] = blend[...].reshape(frames, ROWS, depth).astype(jnp.bfloat16)
        tile = i * z_count + z

        land, sem = res.at[slot, tile], rrecv_sem.at[slot]

        def body(n, carry):
            to = me ^ (frames - n)
            pltpu.make_async_remote_copy(
                rsend.at[half, to], land, rsend_sem.at[half], sem,
                device_id={"tm": to}, device_id_type=MESH,
            ).start()
            return carry

        lax.fori_loop(1, frames, body, 0)
        pltpu.make_async_copy(rsend.at[half, me], land, sem).start()

    my_rank = (core ^ ((z >> 2) & 1)) * 4 + ((y - z) & 3)
    twice = my_rank == 0

    for i in range(SLOTS):
        swaps[1, i].start()
    spread(0)
    stage(1)
    spread(1)
    for slot in range(1, SLOTS):
        for i in range(SLOTS):
            swaps[slot, i].wait_recv()
            if slot == 1:
                swaps[2, i].start()
            unit = UNITS.index((slot, i))
            stage(unit)
            spread(unit)
    stage(len(UNITS) - 1)
    spread(len(UNITS) - 1)

    for s in range(1, SLOTS):
        pieces = []
        for a in range(3):
            theirs = wrecv[s - 1, :, a].reshape(tiles, ROWS, depth)
            pieces.append(jnp.where(heavy, theirs, own[a, major(s)]))
        spatial(s, pieces)

    temporal(jnp.where(twice, 0, my_rank + 1), 0)

    def swap_back(s):
        pltpu.make_async_copy(res.at[s], res.at[s], rrecv_sem.at[s]).wait()
        bsend[s - 1] = jnp.where(heavy, res[SLOTS + s], res[s])
        back = pltpu.make_async_remote_copy(
            bsend.at[s - 1], res.at[2 * SLOTS - 1 + s], bsend_sem.at[s - 1], brecv_sem.at[s - 1],
            device_id=partner, device_id_type=MESH,
        )
        back.start()
        return back

    @pl.when(twice)
    def _():
        temporal(jnp.int32(1), 1)

    backs = [swap_back(1), swap_back(2)]
    pltpu.make_async_copy(res.at[0], res.at[0], rrecv_sem.at[0]).wait()

    for swap in swaps.values():
        swap.wait_send()

    def drain(buffer, sem):
        pltpu.make_async_copy(buffer, buffer, sem).wait()

    drain(rsend.at[0, pl.ds(0, frames - 1)], rsend_sem.at[0])

    @pl.when(twice)
    def _():
        drain(rsend.at[1, pl.ds(0, frames - 1)], rsend_sem.at[1])
        drain(tsend.at[pl.ds(0, len(UNITS) * z_count - 2)], tsend_sem)

    @pl.when(jnp.logical_not(twice))
    def _():
        drain(tsend.at[pl.ds(0, len(UNITS) * z_count - 1)], tsend_sem)

    for back in backs:
        back.wait()

    for h in range(heads):
        k = h - (odd < h).astype(jnp.int32)
        from_major = jnp.where(k < SLOTS, jnp.where(heavy, k, SLOTS + k), SLOTS + k)
        from_odd = jnp.where(heavy, SLOTS, 0)
        out_ref[h] = res[jnp.where(odd == h, from_odd, from_major)]


def per_device(queries, key_vectors, value_vectors, head_class, frame_mask):
    _, patches, heads, depth = queries.shape
    frames = lax.axis_size("tm")
    tiles = patches // ROWS
    by_head = [
        jnp.transpose(a[0], (1, 0, 2)).reshape(heads, tiles, ROWS, depth)
        for a in (queries, key_vectors, value_vectors)
    ]
    bf16, f32 = jnp.bfloat16, jnp.float32
    tile = (ROWS, depth)
    dma = pltpu.SemaphoreType.DMA
    out = pl.pallas_call(
        kernel,
        out_shape=jax.ShapeDtypeStruct((heads, tiles, ROWS, depth), bf16),
        in_specs=[pl.BlockSpec(memory_space=pltpu.HBM)] * 5,
        out_specs=pl.BlockSpec(memory_space=pltpu.VMEM),
        scratch_shapes=[
            pltpu.SMEM(head_class.shape, jnp.int32),
            pltpu.SMEM(frame_mask.shape, jnp.int32),
            pltpu.VMEM((3, heads, tiles) + tile, bf16),
            pltpu.VMEM((SLOTS * tiles, 3) + tile, bf16),
            pltpu.VMEM((SLOTS - 1, SLOTS, 3, tiles // SLOTS) + tile, bf16),
            pltpu.VMEM((SLOTS - 1, SLOTS, 3, tiles // SLOTS) + tile, bf16),
            pltpu.VMEM((2, frames, 3) + tile, bf16),
            pltpu.VMEM((3, frames * ROWS, depth), f32),
            pltpu.VMEM((frames * ROWS, depth), f32),
            pltpu.VMEM((2, frames) + tile, bf16),
            pltpu.VMEM((3 * SLOTS - 1, tiles) + tile, bf16),
            pltpu.VMEM((SLOTS - 1, tiles) + tile, bf16),
            dma((5,)),
            dma((SLOTS - 1, SLOTS)),
            dma((SLOTS - 1, SLOTS)),
            dma,
            dma((2,)),
            dma((2,)),
            dma((SLOTS,)),
            dma((SLOTS - 1,)),
            dma((SLOTS - 1,)),
        ],
        compiler_params=pltpu.CompilerParams(
            collective_id=0, has_side_effects=True, vmem_limit_bytes=40 * 2**20
        ),
        name="split_heads_attention",
    )(head_class, frame_mask, *by_head)
    return jnp.transpose(out.reshape(heads, patches, depth), (1, 0, 2))[None]


def solution(mesh):
    spec = P("tm", None, "head", None)
    return jax.shard_map(
        per_device,
        mesh=mesh,
        in_specs=(spec, spec, spec, P(), P()),
        out_specs=spec,
        check_vma=False,
    )
```

time: 84.7 us -> 82.7 us (0.976)
  Pallas kernels: 79.7 us -> 77.3 us
    pallas_call x1, Pallas kernels: 79.7 us -> 77.3 us  [per_device(): pl.pallas_call(kernel, out_shape=jax.ShapeDtypeStruct((heads, tiles, ROWS...]
where the time goes in v2:
time: 82.7 us; the launch traced here: 82 us
  Pallas kernels  77.3 us (93%)
  local copies, waits for them, and re-layouts  4.69 us (6%)
    pallas_call x1, Pallas kernels, per_device(): pl.pallas_call(kernel, out_shape=jax.ShapeDtypeStruct((heads, tiles, ROWS...  77.3 us
    unnamed x11, local copies, waits for them, and re-layouts  4.69 us

profile of v2, /device:TPU:1, one launch (start us, length us, event | category | flops | bytes accessed | tf_op | source)
XLA Modules:
  0.0 82.0 jit_solution(7323409346856750774)
XLA Ops:
  0.0 0.0 copy-start.3
  0.0 0.0 copy-start.4
  0.0 0.7 copy-done.3
  0.7 0.0 copy-done.4
  0.7 0.0 copy-start
  0.7 1.1 %copy-done = bf16[1,384,6,128]{3,1,2,0:T(8,128)(2,1)S(1)} copy-done((bf16[1,384,6,128]{3,1,2,0:T(8,128)(2,1)S(1)}, bf16[1,384,6,128]{3,1,2,0:T(8,128)(2,1)}, u32[]{:S(2)}) %copy-start) | copy-done | bytes 589848
  1.8 0.0 copy-start.1
  1.8 1.1 %copy-done.1 = bf16[1,384,6,128]{3,1,2,0:T(8,128)(2,1)S(1)} copy-done((bf16[1,384,6,128]{3,1,2,0:T(8,128)(2,1)S(1)}, bf16[1,384,6,128]{3,1,2,0:T(8,128)(2,1)}, u32[]{:S(2)}) %copy-start.1) | copy-done | bytes 589848
  2.8 0.0 copy-start.2
  2.8 1.1 %copy-done.2 = bf16[1,384,6,128]{3,1,2,0:T(8,128)(2,1)S(1)} copy-done((bf16[1,384,6,128]{3,1,2,0:T(8,128)(2,1)S(1)}, bf16[1,384,6,128]{3,1,2,0:T(8,128)(2,1)}, u32[]{:S(2)}) %copy-start.2) | copy-done | bytes 589848
  3.9 77.3 %split_heads_attention.1 = bf16[6,48,8,128]{3,2,1,0:T(8,128)(2,1)S(1)} custom-call(s32[24]{0:T(128)S(1)} %copy-done.4, s32[4,4]{1,0:T(4,128)S(1)} %copy-done.3, bf16[6,48,8,128]{3,2,1,0:T(8,128)(2,1)S(1)} %bitcast.21, bf16[6,48,8,128]{3,2,1,0:T(8,128)(2,1)S(1)} %bitcast.22, bf16[6,48,8,128]{3,2,1,0:T(8,128)(2,1)S(1)} %bitcast.23), custom_call_target="tpu_custom_call" | custom-call | tf_op jit(solution)/shard_map/split_heads_attention/pallas_call | solution.py:279
  81.1 0.8 copy.7
Async XLA Ops:
  0.0 0.7 copy-start.3
  0.0 0.7 copy-start.4
  0.7 1.1 %copy-start = (bf16[1,384,6,128]{3,1,2,0:T(8,128)(2,1)S(1)}, bf16[1,384,6,128]{3,1,2,0:T(8,128)(2,1)}, u32[]{:S(2)}) copy-start(bf16[1,384,6,128]{3,1,2,0:T(8,128)(2,1)} %param.5) | copy-start | bytes 1769476
  1.8 1.1 %copy-start.1 = (bf16[1,384,6,128]{3,1,2,0:T(8,128)(2,1)S(1)}, bf16[1,384,6,128]{3,1,2,0:T(8,128)(2,1)}, u32[]{:S(2)}) copy-start(bf16[1,384,6,128]{3,1,2,0:T(8,128)(2,1)} %param.6) | copy-start | bytes 1769476
  2.8 1.1 %copy-start.2 = (bf16[1,384,6,128]{3,1,2,0:T(8,128)(2,1)S(1)}, bf16[1,384,6,128]{3,1,2,0:T(8,128)(2,1)}, u32[]{:S(2)}) copy-start(bf16[1,384,6,128]{3,1,2,0:T(8,128)(2,1)} %param.7) | copy-start | bytes 1769476

commit v3 on v2

--- a/solution.py
+++ b/solution.py
@@ -67,6 +67,10 @@
     barrier = pltpu.get_barrier_semaphore()
     pl.semaphore_signal(barrier, inc=1, device_id=partner, device_id_type=MESH)
 
+    def step_z(n):
+        step = n * 7
+        return (z + jnp.where(core == 0, step, -step)) & (z_count - 1)
+
     def greet(n, carry):
         pl.semaphore_signal(
             barrier, inc=1, device_id={"tm": me ^ (frames - n)}, device_id_type=MESH
@@ -144,7 +148,7 @@
             ).start()
 
         def body(n, carry):
-            send(z ^ (z_count - n))
+            send(step_z(n))
             return carry
 
         lax.fori_loop(1, z_count, body, 0)
@@ -180,17 +184,34 @@
         rsend[half] = blend[...].reshape(frames, ROWS, depth).astype(jnp.bfloat16)
         tile = i * z_count + z
 
-        land, sem = res.at[slot, tile], rrecv_sem.at[slot]
+        land, sem = res.at[slot, tile], rrecv_sem.at[unit]
+
+        def give(to):
+            @pl.when(to != me)
+            def _():
+                pltpu.make_async_remote_copy(
+                    rsend.at[half, to], land, rsend_sem.at[half], sem,
+                    device_id={"tm": to}, device_id_type=MESH,
+                ).start()
 
         def body(n, carry):
-            to = me ^ (frames - n)
-            pltpu.make_async_remote_copy(
-                rsend.at[half, to], land, rsend_sem.at[half], sem,
-                device_id={"tm": to}, device_id_type=MESH,
-            ).start()
+            zz, turn = step_z(n), n >> 4
+            early = zz < 2
+            late = zz >= 8
+            one = jnp.where(early, 2 * turn, jnp.where(late, jnp.where(turn < 6, turn - 2, 2 * turn - SIDE), turn))
+            two = (early & (turn < 4)) | (late & (turn >= 6))
+
+            @pl.when((one >= 0) & (one < SIDE))
+            def _():
+                give(zz * SIDE + ((me ^ one) & (SIDE - 1)))
+
+            @pl.when(two)
+            def _():
+                give(zz * SIDE + ((me ^ (one + 1)) & (SIDE - 1)))
+
             return carry
 
-        lax.fori_loop(1, frames, body, 0)
+        lax.fori_loop(0, frames, body, 0)
         pltpu.make_async_copy(rsend.at[half, me], land, sem).start()
 
     my_rank = (core ^ ((z >> 2) & 1)) * 4 + ((y - z) & 3)
@@ -221,22 +242,32 @@
 
     temporal(jnp.where(twice, 0, my_rank + 1), 0)
 
-    def swap_back(s):
-        pltpu.make_async_copy(res.at[s], res.at[s], rrecv_sem.at[s]).wait()
-        bsend[s - 1] = jnp.where(heavy, res[SLOTS + s], res[s])
-        back = pltpu.make_async_remote_copy(
-            bsend.at[s - 1], res.at[2 * SLOTS - 1 + s], bsend_sem.at[s - 1], brecv_sem.at[s - 1],
-            device_id=partner, device_id_type=MESH,
-        )
-        back.start()
-        return back
-
     @pl.when(twice)
     def _():
         temporal(jnp.int32(1), 1)
 
-    backs = [swap_back(1), swap_back(2)]
-    pltpu.make_async_copy(res.at[0], res.at[0], rrecv_sem.at[0]).wait()
+    def landed(unit):
+        slot, i = UNITS[unit]
+        part = res.at[slot, unit_rows(i)]
+        pltpu.make_async_copy(part, part, rrecv_sem.at[unit]).wait()
+
+    backs = []
+    for unit, (slot, i) in enumerate(UNITS):
+        if slot > 0:
+            landed(unit)
+            rows = unit_rows(i)
+            bsend[slot - 1, rows] = jnp.where(heavy, res[SLOTS + slot, rows], res[slot, rows])
+            back = pltpu.make_async_remote_copy(
+                bsend.at[slot - 1, rows], res.at[2 * SLOTS - 1 + slot, rows],
+                bsend_sem.at[slot - 1, i], brecv_sem.at[slot - 1, i],
+                device_id=partner, device_id_type=MESH,
+            )
+            back.start()
+            backs.append(back)
+
+    for unit, (slot, _) in enumerate(UNITS):
+        if slot == 0:
+            landed(unit)
 
     for swap in swaps.values():
         swap.wait_send()
@@ -300,9 +331,9 @@
             dma,
             dma((2,)),
             dma((2,)),
-            dma((SLOTS,)),
-            dma((SLOTS - 1,)),
-            dma((SLOTS - 1,)),
+            dma((len(UNITS),)),
+            dma((SLOTS - 1, SLOTS)),
+            dma((SLOTS - 1, SLOTS)),
         ],
         compiler_params=pltpu.CompilerParams(
             collective_id=0, has_side_effects=True, vmem_limit_bytes=40 * 2**20

time: 82.7 us -> 80.1 us (0.969)
  Pallas kernels: 77.3 us -> 75.1 us
    pallas_call x1, Pallas kernels: 77.3 us -> 75.1 us  [per_device(): pl.pallas_call(kernel, out_shape=jax.ShapeDtypeStruct((heads, tiles, ROWS...]
where the time goes in v3:
time: 80.1 us; the launch traced here: 79.8 us
  Pallas kernels  75.1 us (94%)
  local copies, waits for them, and re-layouts  4.69 us (6%)
    pallas_call x1, Pallas kernels, per_device(): pl.pallas_call(kernel, out_shape=jax.ShapeDtypeStruct((heads, tiles, ROWS...  75.1 us
    unnamed x11, local copies, waits for them, and re-layouts  4.69 us

profile of v3, /device:TPU:1, one launch (start us, length us, event | category | flops | bytes accessed | tf_op | source)
XLA Modules:
  0.0 79.8 jit_solution(15753004626053498276)
XLA Ops:
  0.0 0.0 copy-start.3
  0.0 0.0 copy-start.4
  0.0 0.7 copy-done.3
  0.7 0.0 copy-done.4
  0.7 0.0 copy-start
  0.7 1.1 %copy-done = bf16[1,384,6,128]{3,1,2,0:T(8,128)(2,1)S(1)} copy-done((bf16[1,384,6,128]{3,1,2,0:T(8,128)(2,1)S(1)}, bf16[1,384,6,128]{3,1,2,0:T(8,128)(2,1)}, u32[]{:S(2)}) %copy-start) | copy-done | bytes 589848
  1.8 0.0 copy-start.1
  1.8 1.1 %copy-done.1 = bf16[1,384,6,128]{3,1,2,0:T(8,128)(2,1)S(1)} copy-done((bf16[1,384,6,128]{3,1,2,0:T(8,128)(2,1)S(1)}, bf16[1,384,6,128]{3,1,2,0:T(8,128)(2,1)}, u32[]{:S(2)}) %copy-start.1) | copy-done | bytes 589848
  2.8 0.0 copy-start.2
  2.8 1.1 %copy-done.2 = bf16[1,384,6,128]{3,1,2,0:T(8,128)(2,1)S(1)} copy-done((bf16[1,384,6,128]{3,1,2,0:T(8,128)(2,1)S(1)}, bf16[1,384,6,128]{3,1,2,0:T(8,128)(2,1)}, u32[]{:S(2)}) %copy-start.2) | copy-done | bytes 589848
  3.9 75.1 %split_heads_attention.1 = bf16[6,48,8,128]{3,2,1,0:T(8,128)(2,1)S(1)} custom-call(s32[24]{0:T(128)S(1)} %copy-done.4, s32[4,4]{1,0:T(4,128)S(1)} %copy-done.3, bf16[6,48,8,128]{3,2,1,0:T(8,128)(2,1)S(1)} %bitcast.21, bf16[6,48,8,128]{3,2,1,0:T(8,128)(2,1)S(1)} %bitcast.22, bf16[6,48,8,128]{3,2,1,0:T(8,128)(2,1)S(1)} %bitcast.23), custom_call_target="tpu_custom_call" | custom-call | tf_op jit(solution)/shard_map/split_heads_attention/pallas_call | solution.py:310
  79.0 0.8 %copy.7 = bf16[1,384,6,128]{3,1,2,0:T(8,128)(2,1)} copy(bf16[1,384,6,128]{3,1,2,0:T(8,128)(2,1)S(1)} %bitcast.20) | data formatting | bytes 1179648
Async XLA Ops:
  0.0 0.7 copy-start.3
  0.0 0.7 copy-start.4
  0.7 1.1 %copy-start = (bf16[1,384,6,128]{3,1,2,0:T(8,128)(2,1)S(1)}, bf16[1,384,6,128]{3,1,2,0:T(8,128)(2,1)}, u32[]{:S(2)}) copy-start(bf16[1,384,6,128]{3,1,2,0:T(8,128)(2,1)} %param.5) | copy-start | bytes 1769476
  1.8 1.1 %copy-start.1 = (bf16[1,384,6,128]{3,1,2,0:T(8,128)(2,1)S(1)}, bf16[1,384,6,128]{3,1,2,0:T(8,128)(2,1)}, u32[]{:S(2)}) copy-start(bf16[1,384,6,128]{3,1,2,0:T(8,128)(2,1)} %param.6) | copy-start | bytes 1769476
  2.8 1.1 %copy-start.2 = (bf16[1,384,6,128]{3,1,2,0:T(8,128)(2,1)S(1)}, bf16[1,384,6,128]{3,1,2,0:T(8,128)(2,1)}, u32[]{:S(2)}) copy-start(bf16[1,384,6,128]{3,1,2,0:T(8,128)(2,1)} %param.7) | copy-start | bytes 1769476

commit v4 on v3

--- a/solution.py
+++ b/solution.py
@@ -72,12 +72,18 @@
         return (z + jnp.where(core == 0, step, -step)) & (z_count - 1)
 
     def greet(n, carry):
+        turn = n >> 3
+        half = (turn + 1) >> 1
+        zz = (z + z_count // 2 + jnp.where((turn & 1) == 1, -half, half)) & (z_count - 1)
         pl.semaphore_signal(
-            barrier, inc=1, device_id={"tm": me ^ (frames - n)}, device_id_type=MESH
+            barrier,
+            inc=1,
+            device_id={"tm": zz * SIDE + ((me ^ (SIDE - 1 - (n & (SIDE - 1)))) & (SIDE - 1))},
+            device_id_type=MESH,
         )
         return carry
 
-    lax.fori_loop(1, frames, greet, 0)
+    lax.fori_loop(0, frames - 1, greet, 0)
 
     for load in loads:
         load.wait()

time: 80.1 us -> 79.6 us (level)
  no operation moved by 1% of the time
where the time goes in v4:
time: 79.6 us; the launch traced here: 79.3 us
  Pallas kernels  74.6 us (94%)
  local copies, waits for them, and re-layouts  4.69 us (6%)
    pallas_call x1, Pallas kernels, per_device(): pl.pallas_call(kernel, out_shape=jax.ShapeDtypeStruct((heads, tiles, ROWS...  74.6 us
    unnamed x11, local copies, waits for them, and re-layouts  4.69 us

profile of v4, /device:TPU:1, one launch (start us, length us, event | category | flops | bytes accessed | tf_op | source)
XLA Modules:
  0.0 79.3 jit_solution(6091554767526056670)
XLA Ops:
  0.0 0.0 copy-start.3
  0.0 0.0 copy-start.4
  0.0 0.7 copy-done.3
  0.7 0.0 copy-done.4
  0.7 0.0 copy-start
  0.7 1.1 %copy-done = bf16[1,384,6,128]{3,1,2,0:T(8,128)(2,1)S(1)} copy-done((bf16[1,384,6,128]{3,1,2,0:T(8,128)(2,1)S(1)}, bf16[1,384,6,128]{3,1,2,0:T(8,128)(2,1)}, u32[]{:S(2)}) %copy-start) | copy-done | bytes 589848
  1.8 0.0 copy-start.1
  1.8 1.1 %copy-done.1 = bf16[1,384,6,128]{3,1,2,0:T(8,128)(2,1)S(1)} copy-done((bf16[1,384,6,128]{3,1,2,0:T(8,128)(2,1)S(1)}, bf16[1,384,6,128]{3,1,2,0:T(8,128)(2,1)}, u32[]{:S(2)}) %copy-start.1) | copy-done | bytes 589848
  2.8 0.0 copy-start.2
  2.8 1.1 %copy-done.2 = bf16[1,384,6,128]{3,1,2,0:T(8,128)(2,1)S(1)} copy-done((bf16[1,384,6,128]{3,1,2,0:T(8,128)(2,1)S(1)}, bf16[1,384,6,128]{3,1,2,0:T(8,128)(2,1)}, u32[]{:S(2)}) %copy-start.2) | copy-done | bytes 589848
  3.9 74.6 %split_heads_attention.1 = bf16[6,48,8,128]{3,2,1,0:T(8,128)(2,1)S(1)} custom-call(s32[24]{0:T(128)S(1)} %copy-done.4, s32[4,4]{1,0:T(4,128)S(1)} %copy-done.3, bf16[6,48,8,128]{3,2,1,0:T(8,128)(2,1)S(1)} %bitcast.21, bf16[6,48,8,128]{3,2,1,0:T(8,128)(2,1)S(1)} %bitcast.22, bf16[6,48,8,128]{3,2,1,0:T(8,128)(2,1)S(1)} %bitcast.23), custom_call_target="tpu_custom_call" | custom-call | tf_op jit(solution)/shard_map/split_heads_attention/pallas_call | solution.py:316
  78.5 0.8 %copy.7 = bf16[1,384,6,128]{3,1,2,0:T(8,128)(2,1)} copy(bf16[1,384,6,128]{3,1,2,0:T(8,128)(2,1)S(1)} %bitcast.20) | data formatting | bytes 1179648
Async XLA Ops:
  0.0 0.7 copy-start.3
  0.0 0.7 copy-start.4
  0.7 1.1 %copy-start = (bf16[1,384,6,128]{3,1,2,0:T(8,128)(2,1)S(1)}, bf16[1,384,6,128]{3,1,2,0:T(8,128)(2,1)}, u32[]{:S(2)}) copy-start(bf16[1,384,6,128]{3,1,2,0:T(8,128)(2,1)} %param.5) | copy-start | bytes 1769476
  1.8 1.1 %copy-start.1 = (bf16[1,384,6,128]{3,1,2,0:T(8,128)(2,1)S(1)}, bf16[1,384,6,128]{3,1,2,0:T(8,128)(2,1)}, u32[]{:S(2)}) copy-start(bf16[1,384,6,128]{3,1,2,0:T(8,128)(2,1)} %param.6) | copy-start | bytes 1769476
  2.8 1.1 %copy-start.2 = (bf16[1,384,6,128]{3,1,2,0:T(8,128)(2,1)S(1)}, bf16[1,384,6,128]{3,1,2,0:T(8,128)(2,1)}, u32[]{:S(2)}) copy-start(bf16[1,384,6,128]{3,1,2,0:T(8,128)(2,1)} %param.7) | copy-start | bytes 1769476
